TPU v7x, 32 devices: a whole 2x2x4 slice. The times are simulated.
32 devices in a mesh: groups: 2 (over x), row: 4 (over z), col: 4 (over y, core).
Axes of the slice: x: 2, y: 2, z: 4, core: 2. Of those that a mesh axis runs over, the one named last changes fastest.
Arguments:
- height: float32 [4096, 1024], P(('groups', 'row'), 'col'), parts along dimension 0, may hold values from -2.5 to 2.5
- rigidity: float32 [4096, 1024], P(('groups', 'row'), 'col'), parts along dimension 0, may hold values from 0.4 to 1.6
- adhesion: float32 [4096, 1024], P(('groups', 'row'), 'col'), parts along dimension 0, may hold values from 1 to 10
- forcing: bfloat16 [4, 4096, 1024], P(None, ('groups', 'row'), 'col'), parts along dimension 1, may hold values from -6 to 6
Outputs:
- new_height: float32 [4096, 1024], P(('groups', 'row'), 'col'), parts along dimension 0
- velocity_spectrum: float32 [2048, 2, 1024], P(('groups', 'col'), None, 'row'), parts along dimension 0
There are 2 independent parts, one for each index of `groups`. A program takes and returns all parts, laid end to end along the dimension named above; each array names one. Nothing has to cross between parts.
All inputs are finite; a program needn't handle non-finite values.
Results may differ from a plain program's by a relative error of at most 0.0067.
Values may be sent and summed in bfloat16 or wider, within the bound.
A program may use at most 128 MiB of HBM per device.

v0:
```python
import math

import jax
import jax.numpy as jnp
from jax import lax
from jax.sharding import PartitionSpec as P

step_size = 0.008
wave_floor = 0.25


def extended(cells, sides, width):
    for axis, dim in sides:
        count = lax.axis_size(axis)
        head = lax.slice_in_dim(cells, 0, width, axis=dim)
        tail = lax.slice_in_dim(cells, cells.shape[dim] - width, cells.shape[dim], axis=dim)
        cells = jnp.concatenate(
            [
                lax.ppermute(tail, axis, [(i, (i + 1) % count) for i in range(count)]),
                cells,
                lax.ppermute(head, axis, [((i + 1) % count, i) for i in range(count)]),
            ],
            axis=dim,
        )
    return cells


def lap_four(grid):
    middle = grid[2:-2, 2:-2]
    first_dir = (
        -grid[:-4, 2:-2]
        + 16.0 * grid[1:-3, 2:-2]
        - 30.0 * middle
        + 16.0 * grid[3:-1, 2:-2]
        - grid[4:, 2:-2]
    )
    second_dir = (
        -grid[2:-2, :-4]
        + 16.0 * grid[2:-2, 1:-3]
        - 30.0 * middle
        + 16.0 * grid[2:-2, 3:-1]
        - grid[2:-2, 4:]
    )
    return (first_dir + second_dir) / 12.0


def slope_sq(grid):
    slope_rows = (
        grid[:-4, 2:-2] - 8.0 * grid[1:-3, 2:-2] + 8.0 * grid[3:-1, 2:-2] - grid[4:, 2:-2]
    ) / 12.0
    slope_cols = (
        grid[2:-2, :-4] - 8.0 * grid[2:-2, 1:-3] + 8.0 * grid[2:-2, 3:-1] - grid[2:-2, 4:]
    ) / 12.0
    return slope_rows * slope_rows + slope_cols * slope_cols


def substep(padded, rigidity, adhesion, noise_now):
    metric = 1.0 + slope_sq(padded)
    curvature = lap_four(padded) / (metric * jnp.sqrt(metric))
    bending = rigidity * lap_four(curvature)
    center = padded[4:-4, 4:-4]
    binding = adhesion * center * jnp.exp(-0.5 * center * center)
    return center + step_size * (noise_now - bending - binding)


def phase_table(row_start, extent, col_start, span_len, period):
    coarse_count = -(-extent // 64)
    col_ids = col_start + lax.iota(jnp.int32, span_len)[None, :]
    coarse_ids = row_start + 64 * lax.iota(jnp.int32, coarse_count)[:, None]
    fine_ids = lax.iota(jnp.int32, 64)[:, None]
    unit = 2.0 * math.pi / period
    coarse_angle = (coarse_ids * col_ids % period).astype(jnp.float32) * unit
    fine_angle = (fine_ids * col_ids % period).astype(jnp.float32) * unit
    cos_p = jnp.cos(coarse_angle)[:, None, :]
    sin_p = jnp.sin(coarse_angle)[:, None, :]
    cos_q = jnp.cos(fine_angle)[None, :, :]
    sin_q = jnp.sin(fine_angle)[None, :, :]
    cosines = (cos_p * cos_q - sin_p * sin_q).reshape(coarse_count * 64, span_len)
    sines = (sin_p * cos_q + cos_p * sin_q).reshape(coarse_count * 64, span_len)
    return (cosines.astype(jnp.bfloat16), sines.astype(jnp.bfloat16))


def wave_terms(start, extent, operand, col_start, span_len, period, half_width):
    cosines, sines = phase_table(start, extent, col_start, span_len, period)
    direct = jnp.dot(cosines, operand, preferred_element_type=jnp.float32)
    turned = jnp.dot(sines, operand, preferred_element_type=jnp.float32)
    real_part = direct[:, :half_width] + turned[:, half_width:]
    sine_part = direct[:, half_width:] - turned[:, :half_width]
    return jnp.concatenate([real_part, sine_part], axis=1)


def on_device(height, rigidity, adhesion, forcing):
    local_rows, local_cols = height.shape
    substeps = forcing.shape[0]
    depth_all = 4 * substeps
    stacked = jnp.concatenate(
        [height[None], rigidity[None], adhesion[None], forcing.astype(jnp.float32)], axis=0
    )
    widened = extended(stacked, (("row", 1), ("col", 2)), depth_all)
    surface = widened[0]
    for iteration in range(substeps):
        margin = depth_all - 4 * (iteration + 1)
        lower_edge = depth_all - margin
        inner_part = widened[
            :,
            lower_edge : lower_edge + local_rows + 2 * margin,
            lower_edge : lower_edge + local_cols + 2 * margin,
        ]
        surface = substep(surface, inner_part[1], inner_part[2], inner_part[3 + iteration])
    velocity = ((surface - height) / (substeps * step_size)).astype(jnp.bfloat16)
    row_count = lax.axis_size("row")
    col_count = lax.axis_size("col")
    full_rows = local_rows * row_count
    full_cols = local_cols * col_count
    half_rows = full_rows // 2
    columns = lax.all_to_all(velocity, "row", split_axis=1, concat_axis=0, tiled=True)
    block_len = max(512, -(-half_rows // 8))
    real_parts = []
    sine_parts = []
    for offset in range(0, half_rows, block_len):
        extent = min(block_len, half_rows - offset)
        cosines, sines = phase_table(offset, extent, 0, full_rows, full_rows)
        real_parts.append(
            lax.dot_general(
                columns, cosines, (((0,), (1,)), ((), ())), preferred_element_type=jnp.float32
            )
        )
        sine_parts.append(
            -lax.dot_general(
                columns, sines, (((0,), (1,)), ((), ())), preferred_element_type=jnp.float32
            )
        )
    transformed = jnp.stack(
        [jnp.concatenate(real_parts, axis=1), jnp.concatenate(sine_parts, axis=1)], axis=1
    ).astype(jnp.bfloat16)
    mode_slab = lax.all_to_all(transformed, "row", split_axis=2, concat_axis=0, tiled=True)
    local_modes = mode_slab.shape[2]
    col_start = lax.axis_index("col") * local_cols
    flattened = mode_slab.reshape(local_cols, 2 * local_modes)
    summed = lax.psum_scatter(
        wave_terms(
            jnp.int32(0),
            local_cols * lax.axis_size("col"),
            flattened,
            col_start,
            local_cols,
            full_cols,
            local_modes,
        ),
        "col",
        scatter_dimension=0,
        tiled=True,
    )
    spectrum = summed.reshape(local_cols, 2, local_modes)
    wave_y = col_start + lax.iota(jnp.int32, local_cols)
    signed = jnp.where(wave_y < full_cols // 2, wave_y, wave_y - full_cols)
    angle_y = signed.astype(jnp.float32) * (2.0 * math.pi / full_cols)
    wave_x = lax.axis_index("row") * local_modes + lax.iota(jnp.int32, local_modes)
    angle_x = wave_x.astype(jnp.float32) * (2.0 * math.pi / full_rows)
    squared = angle_y[:, None] * angle_y[:, None] + angle_x[None, :] * angle_x[None, :]
    mobility = 1.0 / (2.0 * jnp.sqrt(squared + wave_floor)) / math.sqrt(full_rows * full_cols)
    return (surface, spectrum * mobility[:, None, :])


def solution(mesh):
    in_specs = (
        P(("groups", "row"), "col"),
        P(("groups", "row"), "col"),
        P(("groups", "row"), "col"),
        P(None, ("groups", "row"), "col"),
    )
    out_specs = (P(("groups", "row"), "col"), P(("groups", "col"), None, "row"))
    return jax.shard_map(
        on_device, mesh=mesh, in_specs=in_specs, out_specs=out_specs, check_vma=False
    )
```

profile of v0, /device:TPU:1, one launch (start us, length us, event | category | flops | bytes accessed | tf_op | source)
XLA Modules:
  0.0 140.5 jit_solution(11616309806258613632)
XLA Ops:
  7.2 1.5 %copy.21 = bf16[4,512,256]{1,2,0:T(8,128)(2,1)S(1)} copy(bf16[4,512,256]{2,1,0:T(8,128)(2,1)} %param.7) | data formatting | bytes 2097152 | tf_op args[3]
  8.7 0.3 convert_element_type.154
  9.0 1.2 copy.18
  10.2 1.2 copy.19
  11.4 2.0 %copy.20 = f32[512,256]{0,1:T(8,128)} copy(f32[512,256]{1,0:T(8,128)} %param.6) | data formatting | bytes 1048576 | tf_op args[2]
  13.5 2.5 %pad_maximum_fusion.5 = (f32[7,16,256]{1,2,0:T(8,128)}, f32[7,16,256]{1,2,0:T(8,128)}) fusion(f32[4,512,256]{1,2,0:T(8,128)S(1)} %convert_element_type.154, f32[1,512,256]{1,2,0:T(8,128)} %bitcast.92, f32[1,512,256]{1,2,0:T(8,128)S(1)} %bitcast.89, f32[1,512,256]{1,2,0:T(8,128)S(1)} %bitcast.86), kind=kLoop, calls=%fused_computation.26 | loop fusion | flops 172032 | bytes 3899392 | tf_op jit(solution)/shard_map/slice | solution.py:16
  16.0 1.4 %copy.22 = f32[7,16,256]{2,1,0:T(8,128)S(1)} copy(f32[7,16,256]{1,2,0:T(8,128)} %get-tuple-element.12) | data formatting | bytes 229376 | tf_op jit(solution)/shard_map/slice | solution.py:16
  17.5 2.2 %collective-permute-start = (f32[7,16,256]{2,1,0:T(8,128)S(1)}, f32[7,16,256]{2,1,0:T(8,128)}, u32[]{:S(2)}, u32[]{:S(2)}) collective-permute-start(f32[7,16,256]{2,1,0:T(8,128)S(1)} %copy.22), channel_id=1, source_target_pairs={{0,4},{4,8},{8,12},{12,0},{1,5},{5,9},{9,13},{13,1},{2,6},{6,10},{... | collective-permute-start | bytes 344072 | tf_op jit(solution)/shard_map/ppermute | solution.py:19
  19.6 2.1 %copy.23 = f32[7,16,256]{2,1,0:T(8,128)} copy(f32[7,16,256]{1,2,0:T(8,128)} %get-tuple-element.13) | data formatting | bytes 229376 | tf_op jit(solution)/shard_map/slice | solution.py:15
  21.7 2.0 %collective-permute-start.1 = (f32[7,16,256]{2,1,0:T(8,128)}, f32[7,16,256]{2,1,0:T(8,128)}, u32[]{:S(2)}, u32[]{:S(2)}) collective-permute-start(f32[7,16,256]{2,1,0:T(8,128)} %copy.23), channel_id=1, source_target_pairs={{4,0},{8,4},{12,8},{0,12},{5,1},{9,5},{13,9},{1,13},{6,2},{10,6},{... | collective-permute-start | bytes 344072 | tf_op jit(solution)/shard_map/ppermute | solution.py:21
  23.8 0.6 fusion.96
  24.4 2.9 %fusion.75 = (f32[64,2048]{1,0:T(8,128)}, f32[64,2048]{1,0:T(8,128)}) fusion(), kind=kLoop, calls=%fused_computation.165 | loop fusion | flops 1835008 | bytes 1048576 | tf_op jit(solution)/shard_map/sin | solution.py:77
  27.2 0.0 collective-permute-done
  27.2 2.2 %copy.24 = f32[7,16,256]{1,2,0:T(8,128)} copy(f32[7,16,256]{2,1,0:T(8,128)} %collective-permute-done) | data formatting | bytes 229376 | tf_op jit(solution)/shard_map/ppermute | solution.py:19
  29.5 0.0 collective-permute-done.1
  29.5 2.1 %copy.25 = f32[7,16,256]{1,2,0:T(8,128)} copy(f32[7,16,256]{2,1,0:T(8,128)} %collective-permute-done.1) | data formatting | bytes 229376 | tf_op jit(solution)/shard_map/ppermute | solution.py:21
  31.6 1.2 pad_maximum_fusion.11
  32.8 2.3 %collective-permute-start.2 = (f32[7,544,16]{1,2,0:T(8,128)S(1)}, f32[7,544,16]{1,2,0:T(8,128)S(1)}, u32[]{:S(2)}, u32[]{:S(2)}) collective-permute-start(f32[7,544,16]{1,2,0:T(8,128)S(1)} %get-tuple-element.8), channel_id=1, source_target_pairs={{0,1},{1,2},{2,3},{3,0},{4,5},{5,6},{6,7},{7,4},{8,9},{9,10},{10,1... | collective-permute-start | bytes 731144 | tf_op jit(solution)/shard_map/ppermute | solution.py:19
  35.2 0.0 collective-permute-start.3
  35.2 0.0 copy-done.6
  35.2 0.0 copy-done.7
  35.2 0.0 copy-start
  35.2 0.0 copy-start.3
  35.2 0.0 copy-start.4
  35.2 4.5 %subtract_convert_fusion.1 = (bf16[8,64,2048]{2,1,0:T(8,128)(2,1)}, bf16[8,64,2048]{2,1,0:T(8,128)(2,1)}, bf16[8,64,2048]{2,1,0:T(8,128)(2,1)}, bf16[8,64,2048]{2,1,0:T(8,128)(2,1)}) fusion(f32[64,2048]{1,0:T(8,128)S(1)} %copy-done.6, f32[8,2048]{1,0:T(8,128)S(1)} %get-tuple-element.32, f32[64,2048]{1,0:T(8,128)S(1)} %copy-done.7, ...), kind=kLoop, calls=%fused_computation.4 | loop fusion | flops 16777216 | bytes 9699328 | tf_op jit(solution)/shard_map/convert_element_type | solution.py:80
  39.7 1.5 %collective-permute-done.2 = f32[7,544,16]{1,2,0:T(8,128)S(1)} collective-permute-done((f32[7,544,16]{1,2,0:T(8,128)S(1)}, f32[7,544,16]{1,2,0:T(8,128)S(1)}, u32[]{:S(2)}, u32[]{:S(2)}) %collective-permute-start.2) | collective-permute-done | bytes 243744 | tf_op jit(solution)/shard_map/ppermute | solution.py:19
  41.3 1.0 collective-permute-done.3
  42.3 4.4 %pad_maximum_fusion = f32[7,544,288]{1,2,0:T(8,128)S(1)} fusion(f32[7,544,16]{1,2,0:T(8,128)S(1)} %collective-permute-done.3, f32[7,16,256]{1,2,0:T(8,128)S(1)} %copy-done.4, f32[4,512,256]{1,2,0:T(8,128)S(1)} %convert_element_type.154, f32[1,512,256]{1,2,0:T(8,128)S(1)} %bitcast.94, f32[1,512,256]{1,2,0:T(8,128)S(1)} %bitcast.91, ...), kind=kLoop, calls=%fused_computation | loop fusion | flops 7676928 | bytes 8773632 | tf_op jit(solution)/shard_map/concatenate | solution.py:17
  46.8 1.8 %fusion.2 = f32[540,284]{0,1:T(8,128)S(1)} fusion(f32[544,288]{0,1:T(8,128)S(1)} %slice_bitcast_fusion), kind=kLoop, calls=%fused_computation.31 | loop fusion | flops 5367600 | bytes 6134400 | tf_op jit(solution)/shard_map/div | solution.py:59
  48.6 2.6 %fusion.7 = f32[536,280]{0,1:T(8,128)S(1)} fusion(f32[7,544,288]{1,2,0:T(8,128)S(1)} %pad_maximum_fusion, f32[540,284]{0,1:T(8,128)S(1)} %fusion.2, f32[544,288]{0,1:T(8,128)S(1)} %slice_bitcast_fusion), kind=kLoop, calls=%fused_computation.38 | loop fusion | flops 3902080 | bytes 8404480 | tf_op jit(solution)/shard_map/add | solution.py:63
  51.2 1.8 %fusion.8 = f32[532,276]{0,1:T(8,128)S(1)} fusion(f32[536,280]{0,1:T(8,128)S(1)} %fusion.7), kind=kLoop, calls=%fused_computation.39 | loop fusion | flops 5139120 | bytes 5873280 | tf_op jit(solution)/shard_map/div | solution.py:59
  53.0 2.3 %fusion.24 = f32[528,272]{0,1:T(8,128)S(1)} fusion(f32[7,544,288]{1,2,0:T(8,128)S(1)} %pad_maximum_fusion, f32[532,276]{0,1:T(8,128)S(1)} %fusion.8, f32[536,280]{0,1:T(8,128)S(1)} %fusion.7), kind=kLoop, calls=%fused_computation.68 | loop fusion | flops 3734016 | bytes 8042496 | tf_op jit(solution)/shard_map/add | solution.py:63
  55.3 1.7 %fusion.25 = f32[524,268]{0,1:T(8,128)S(1)} fusion(f32[528,272]{0,1:T(8,128)S(1)} %fusion.24), kind=kLoop, calls=%fused_computation.69 | loop fusion | flops 4915120 | bytes 5617280 | tf_op jit(solution)/shard_map/div | solution.py:59
  57.1 2.4 %fusion.41 = f32[520,264]{0,1:T(8,128)S(1)} fusion(f32[7,544,288]{1,2,0:T(8,128)S(1)} %pad_maximum_fusion, f32[524,268]{0,1:T(8,128)S(1)} %fusion.25, f32[528,272]{0,1:T(8,128)S(1)} %fusion.24), kind=kLoop, calls=%fused_computation.98 | loop fusion | flops 3569280 | bytes 7687680 | tf_op jit(solution)/shard_map/add | solution.py:63
  59.5 1.7 %fusion.42 = f32[516,260]{0,1:T(8,128)S(1)} fusion(f32[520,264]{0,1:T(8,128)S(1)} %fusion.41), kind=kLoop, calls=%fused_computation.99 | loop fusion | flops 4695600 | bytes 5366400 | tf_op jit(solution)/shard_map/div | solution.py:59
  61.1 2.2 %multiply_convert_fusion = (bf16[512,256]{0,1:T(8,128)(2,1)}, f32[512,256]{0,1:T(8,128)}) fusion(f32[512,256]{0,1:T(8,128)S(1)} %copy.18, f32[512,256]{0,1:T(8,128)S(1)} %copy-done, f32[512,256]{0,1:T(8,128)S(1)} %copy.19, f32[516,260]{0,1:T(8,128)S(1)} %fusion.42, f32[4,512,256]{1,2,0:T(8,128)S(1)} %convert_element_type.154, f32[520,264]{0,1:T(8,128)S(1)} %fusion.41), kind=kLoop, calls=%fused_computation.154 | loop fusion | flops 3801088 | bytes 8126464 | tf_op jit(solution)/shard_map/convert_element_type | solution.py:110
  63.4 3.5 %all-to-all-start = ((bf16[512,4,64]{0,2,1:T(8,128)(2,1)}), bf16[512,4,64]{0,2,1:T(8,128)(2,1)S(1)}, u32[]{:S(2)}, u32[]{:S(2)}) async-start(bf16[512,4,64]{0,2,1:T(8,128)(2,1)} %bitcast.15), calls=%async_computation | async-start | bytes 524288 | tf_op jit(solution)/shard_map/all_to_all | solution.py:116
  66.9 0.3 fusion.100
  67.2 8.8 %all-to-all-done = bf16[512,4,64]{0,2,1:T(8,128)(2,1)S(1)} async-done(((bf16[512,4,64]{0,2,1:T(8,128)(2,1)}), bf16[512,4,64]{0,2,1:T(8,128)(2,1)S(1)}, u32[]{:S(2)}, u32[]{:S(2)}) %all-to-all-start) | async-done | bytes 262176 | tf_op jit(solution)/shard_map/all_to_all | solution.py:116
  76.1 2.5 %convolution_convert_fusion = bf16[64,512]{1,0:T(8,128)(2,1)S(1)} fusion(bf16[2048,64]{0,1:T(8,128)(2,1)S(1)} %bitcast.99, bf16[512,2048]{1,0:T(8,128)(2,1)} %bitcast.98), kind=kOutput, calls=%fused_computation.10 | convolution fusion | flops 134250496 | bytes 2424832 | tf_op jit(solution)/shard_map/dot_general | solution.py:124
  78.6 2.4 %convolution_convert_fusion.1 = bf16[64,512]{1,0:T(8,128)(2,1)S(1)} fusion(bf16[2048,64]{0,1:T(8,128)(2,1)S(1)} %bitcast.100, bf16[512,2048]{1,0:T(8,128)(2,1)} %bitcast.97), kind=kOutput, calls=%fused_computation.11 | convolution fusion | flops 134250496 | bytes 2424832 | tf_op jit(solution)/shard_map/dot_general | solution.py:124
  80.9 0.0 copy-done.2
  80.9 0.8 fusion
  81.7 0.8 fusion.1
  82.5 0.4 copy.30
  82.9 1.1 reshape.450
  84.0 3.4 %all-to-all-start.1 = ((bf16[4,2,16384]{2,1,0:T(2,128)(2,1)}), bf16[4,2,16384]{2,1,0:T(2,128)(2,1)S(1)}, u32[]{:S(2)}, u32[]{:S(2)}) async-start(bf16[4,2,16384]{2,1,0:T(2,128)(2,1)} %reshape.450), calls=%async_computation.1 | async-start | bytes 524288 | tf_op jit(solution)/shard_map/all_to_all | solution.py:136
  87.4 0.0 reduce-scatter.2.cloned.1.call-start
  87.5 0.2 fusion.105
  87.6 0.3 subtract_convert_fusion.2
  88.0 6.8 %all-to-all-done.1 = bf16[4,2,16384]{2,1,0:T(2,128)(2,1)S(1)} async-done(((bf16[4,2,16384]{2,1,0:T(2,128)(2,1)}), bf16[4,2,16384]{2,1,0:T(2,128)(2,1)S(1)}, u32[]{:S(2)}, u32[]{:S(2)}) %all-to-all-start.1) | async-done | bytes 262176 | tf_op jit(solution)/shard_map/all_to_all | solution.py:136
  94.8 0.3 reshape.451
  95.2 0.4 copy.31
  95.6 0.5 fusion.110
  96.1 0.5 fusion.111
  96.6 0.6 slice_add_fusion
  97.2 0.0 copy-start.5
  97.2 1.5 %pad_maximum_fusion.1 = f32[1024,512]{0,1:T(8,128)} fusion(f32[1024,256]{0,1:T(8,128)S(1)} %get-tuple-element.11, f32[1024,256]{0,1:T(8,128)S(1)} %get-tuple-element.10), kind=kLoop, calls=%fused_computation.5 | loop fusion | flops 524288 | bytes 4194304 | tf_op jit(solution)/shard_map/concatenate | solution.py:89
  98.6 0.0 reduce-scatter.2.cloned.1.call-update
  98.7 0.2 divide_multiply_fusion
  98.9 1.0 copy.33
  99.9 31.4 %reduce-scatter.2.cloned.1.call-done = f32[256,512]{0,1:T(8,128)} async-done(((f32[1024,512]{0,1:T(8,128)}), f32[256,512]{0,1:T(8,128)}) %reduce-scatter.2.cloned.1.call-update) | async-done | bytes 524304 | tf_op jit(solution)/shard_map/reduce_scatter | solution.py:140
  131.3 1.3 copy.32
  132.6 1.1 broadcast_multiply_fusion
  (20 shorter events, 0.2 us)
Async XLA Ops:
  17.5 9.8 %collective-permute-start = (f32[7,16,256]{2,1,0:T(8,128)S(1)}, f32[7,16,256]{2,1,0:T(8,128)}, u32[]{:S(2)}, u32[]{:S(2)}) collective-permute-start(f32[7,16,256]{2,1,0:T(8,128)S(1)} %copy.22), channel_id=1, source_target_pairs={{0,4},{4,8},{8,12},{12,0},{1,5},{5,9},{9,13},{13,1},{2,6},{6,10},{... | collective-permute-start | bytes 344072 | tf_op jit(solution)/shard_map/ppermute | solution.py:19
  21.7 7.7 %collective-permute-start.1 = (f32[7,16,256]{2,1,0:T(8,128)}, f32[7,16,256]{2,1,0:T(8,128)}, u32[]{:S(2)}, u32[]{:S(2)}) collective-permute-start(f32[7,16,256]{2,1,0:T(8,128)} %copy.23), channel_id=1, source_target_pairs={{4,0},{8,4},{12,8},{0,12},{5,1},{9,5},{13,9},{1,13},{6,2},{10,6},{... | collective-permute-start | bytes 344072 | tf_op jit(solution)/shard_map/ppermute | solution.py:21
  31.6 3.6 %copy-start.6 = (f32[64,2048]{1,0:T(8,128)S(1)}, f32[64,2048]{1,0:T(8,128)}, u32[]{:S(2)}) copy-start(f32[64,2048]{1,0:T(8,128)} %get-tuple-element.30) | copy-start | bytes 1572868
  31.6 3.6 %copy-start.7 = (f32[64,2048]{1,0:T(8,128)S(1)}, f32[64,2048]{1,0:T(8,128)}, u32[]{:S(2)}) copy-start(f32[64,2048]{1,0:T(8,128)} %get-tuple-element.31) | copy-start | bytes 1572868
  32.8 8.4 %collective-permute-start.2 = (f32[7,544,16]{1,2,0:T(8,128)S(1)}, f32[7,544,16]{1,2,0:T(8,128)S(1)}, u32[]{:S(2)}, u32[]{:S(2)}) collective-permute-start(f32[7,544,16]{1,2,0:T(8,128)S(1)} %get-tuple-element.8), channel_id=1, source_target_pairs={{0,1},{1,2},{2,3},{3,0},{4,5},{5,6},{6,7},{7,4},{8,9},{9,10},{10,1... | collective-permute-start | bytes 731144 | tf_op jit(solution)/shard_map/ppermute | solution.py:19
  35.2 7.1 %collective-permute-start.3 = (f32[7,544,16]{1,2,0:T(8,128)S(1)}, f32[7,544,16]{1,2,0:T(8,128)S(1)}, u32[]{:S(2)}, u32[]{:S(2)}) collective-permute-start(f32[7,544,16]{1,2,0:T(8,128)S(1)} %get-tuple-element.9), channel_id=1, source_target_pairs={{1,0},{2,1},{3,2},{0,3},{5,4},{6,5},{7,6},{4,7},{9,8},{10,9},{11,1... | collective-permute-start | bytes 731144 | tf_op jit(solution)/shard_map/ppermute | solution.py:21
  35.2 7.1 %copy-start = (f32[512,256]{0,1:T(8,128)S(1)}, f32[512,256]{0,1:T(8,128)}, u32[]{:S(2)}) copy-start(f32[512,256]{0,1:T(8,128)} %copy.20) | copy-start | bytes 1572868
  35.2 7.1 %copy-start.3 = (f32[7,16,256]{1,2,0:T(8,128)S(1)}, f32[7,16,256]{1,2,0:T(8,128)}, u32[]{:S(2)}) copy-start(f32[7,16,256]{1,2,0:T(8,128)} %copy.24) | copy-start | bytes 344068
  35.2 7.1 %copy-start.4 = (f32[7,16,256]{1,2,0:T(8,128)S(1)}, f32[7,16,256]{1,2,0:T(8,128)}, u32[]{:S(2)}) copy-start(f32[7,16,256]{1,2,0:T(8,128)} %copy.25) | copy-start | bytes 344068
  63.4 18.3 %copy-start.1 = (bf16[8,64,2048]{2,1,0:T(8,128)(2,1)S(1)}, bf16[8,64,2048]{2,1,0:T(8,128)(2,1)}, u32[]{:S(2)}) copy-start(bf16[8,64,2048]{2,1,0:T(8,128)(2,1)} %get-tuple-element.18) | copy-start | bytes 6291460
  63.4 12.7 %all-to-all-start = ((bf16[512,4,64]{0,2,1:T(8,128)(2,1)}), bf16[512,4,64]{0,2,1:T(8,128)(2,1)S(1)}, u32[]{:S(2)}, u32[]{:S(2)}) async-start(bf16[512,4,64]{0,2,1:T(8,128)(2,1)} %bitcast.15), calls=%async_computation | async-start | bytes 524288 | tf_op jit(solution)/shard_map/all_to_all | solution.py:116
  76.0 4.9 %copy-start.2 = (bf16[8,64,2048]{2,1,0:T(8,128)(2,1)S(1)}, bf16[8,64,2048]{2,1,0:T(8,128)(2,1)}, u32[]{:S(2)}) copy-start(bf16[8,64,2048]{2,1,0:T(8,128)(2,1)} %get-tuple-element.15) | copy-start | bytes 6291460
  84.0 10.8 %all-to-all-start.1 = ((bf16[4,2,16384]{2,1,0:T(2,128)(2,1)}), bf16[4,2,16384]{2,1,0:T(2,128)(2,1)S(1)}, u32[]{:S(2)}, u32[]{:S(2)}) async-start(bf16[4,2,16384]{2,1,0:T(2,128)(2,1)} %reshape.450), calls=%async_computation.1 | async-start | bytes 524288 | tf_op jit(solution)/shard_map/all_to_all | solution.py:136
  87.4 43.8 %reduce-scatter.2.cloned.1.call-start = ((), (), s32[]{:S(2)}) async-start(), calls=%async_computation.3 | async-start | bytes 2621440 | tf_op jit(solution)/shard_map/reduce_scatter | solution.py:140
  97.2 1.7 %copy-start.5 = (f32[512,256]{0,1:T(8,128)S(1)}, f32[512,256]{0,1:T(8,128)}, u32[]{:S(2)}) copy-start(f32[512,256]{0,1:T(8,128)} %get-tuple-element.7) | copy-start | bytes 1572868
Sparse Core Ops, SparseCore 0:
  98.8 32.4 reduce-scatter.1
where the time goes:
time: 142 us; the launch traced here: 140 us
  waiting for transfers between devices  49.6 us (35%)
  other arithmetic  37.1 us (26%)
  local copies, waits for them, and re-layouts  18.5 us (13%)
  between operations  14.4 us (10%)
  starting transfers between devices  13.5 us (10%)
  matrix products  7.34 us (5%)
    reduce_scatter x1, waiting for transfers between devices, on_device(): lax.psum_scatter(wave_terms(jnp.int32(0), local_cols * lax.axis_size('col...  31.4 us
    all_to_all x1, waiting for transfers between devices, on_device(): lax.all_to_all(velocity, 'row', split_axis=1, concat_axis=0, tiled=True)  8.82 us
    unnamed x24, local copies, waits for them, and re-layouts  8.52 us
    add x3, other arithmetic, substep(): return center + step_size * (noise_now - bending - binding)  7.28 us
    div x4, other arithmetic, substep(): curvature = lap_four(padded) / (metric * jnp.sqrt(metric))  7.01 us
    all_to_all x1, waiting for transfers between devices, on_device(): lax.all_to_all(transformed, 'row', split_axis=2, concat_axis=0, tiled=True)  6.85 us
    dot_general x2, matrix products, on_device(): lax.dot_general(columns, cosines, (((0,), (1,)), ((), ())), preferred_ele...  4.85 us
    convert_element_type x2, other arithmetic, phase_table(): return (cosines.astype(jnp.bfloat16), sines.astype(jnp.bfloat16))  4.84 us
  transfers between devices with their start and end apart: 7, of which 5 were waited for; matrix products, arithmetic and copies ran while one was open for 10% of the time, Pallas kernels for 0%

commit v1 on v0

v1 whole, which is shorter than its diff:
```python
import functools
import math

import jax
import jax.numpy as jnp
from jax import lax
from jax.experimental import pallas as pl
from jax.experimental.pallas import tpu as pltpu
from jax.sharding import PartitionSpec as P

step_size = 0.008
wave_floor = 0.25

LANES = 128
HALO = 16
PAD = 16


def phase_rows(start, modes, period):
    ks = jnp.concatenate(
        [
            8 * lax.iota(jnp.int32, 8),
            lax.iota(jnp.int32, 8),
            start + 64 * lax.iota(jnp.int32, modes // 64),
        ]
    )
    angle = (ks[:, None] * lax.iota(jnp.int32, period)[None, :] % period).astype(jnp.float32) * (
        2.0 * math.pi / period
    )
    return jnp.cos(angle), jnp.sin(angle)


def write_table(cos_ref, sin_ref, width, store):
    rows, period = cos_ref.shape

    def columns(i, carry):
        lanes = pl.ds(pl.multiple_of(i * width, width), width)
        cos_c, sin_c = cos_ref[0:8, lanes], sin_ref[0:8, lanes]
        cos_b, sin_b = cos_ref[8:16, lanes], sin_ref[8:16, lanes]
        for a in range(rows - 16):
            cos_a, sin_a = cos_ref[16 + a : 17 + a, lanes], sin_ref[16 + a : 17 + a, lanes]
            cos_ac = cos_a * cos_c - sin_a * sin_c
            sin_ac = sin_a * cos_c + cos_a * sin_c
            for c in range(0, 8, 2):
                cosines, sines = [], []
                for d in (c, c + 1):
                    cos_r, sin_r = cos_ac[d : d + 1], sin_ac[d : d + 1]
                    cosines.append(cos_r * cos_b - sin_r * sin_b)
                    sines.append(sin_r * cos_b + cos_r * sin_b)
                store(i, 64 * a + 8 * c, jnp.concatenate(cosines, 0), jnp.concatenate(sines, 0))
        return carry

    lax.fori_loop(0, period // width, columns, 0)


def shifted(block, axis):
    size = block.shape[axis]
    return [pltpu.roll(block, shift % size, axis) for shift in (2, 1, -1, -2)]


def second_diff(block, rows, cols):
    ends = rows[0] + rows[3] + cols[0] + cols[3]
    near = rows[1] + rows[2] + cols[1] + cols[2]
    return (16.0 * near - ends - 60.0 * block) * (1.0 / 12.0)


def first_diff(moved):
    return ((moved[0] - moved[3]) + 8.0 * (moved[2] - moved[1])) * (1.0 / 12.0)


def kernel(
    substeps,
    n_row,
    n_col,
    height_ref,
    rigid_ref,
    adhes_ref,
    force_ref,
    cosx_ref,
    sinx_ref,
    cosy_ref,
    siny_ref,
    new_ref,
    wave_ref,
    surf,
    curv,
    extra,
    side_send,
    side_recv,
    edge_send,
    edge_recv,
    table_x,
    table_y,
    vel,
    modes,
    side_ssem,
    side_rsem,
    edge_ssem,
    edge_rsem,
    vel_ssem,
    vel_rsem,
    mode_ssem,
    mode_rsem,
):
    rows, cols = height_ref.shape
    chunks = cols // LANES
    wide = cols + LANES
    me_r = lax.axis_index("row")
    me_c = lax.axis_index("col")
    down = lax.rem(me_r + 1, n_row)
    up = lax.rem(me_r + n_row - 1, n_row)
    right = lax.rem(me_c + 1, n_col)
    left = lax.rem(me_c + n_col - 1, n_col)
    sibling = me_c + 1 - 2 * lax.rem(me_c, 2)
    mesh_ids = pl.DeviceIdType.MESH

    barrier = pltpu.get_barrier_semaphore()
    for target in (down, up):
        pl.semaphore_signal(barrier, inc=1, device_id={"row": target}, device_id_type=mesh_ids)
    for off in range(1, n_col):
        pl.semaphore_signal(
            barrier,
            inc=1,
            device_id={"col": lax.rem(me_c + off, n_col)},
            device_id_type=mesh_ids,
        )

    def send(src, dst, ssem, rsem, where):
        return pltpu.make_async_remote_copy(
            src_ref=src,
            dst_ref=dst,
            send_sem=ssem,
            recv_sem=rsem,
            device_id=where,
            device_id_type=mesh_ids,
        )

    pack_rows = 32

    def pack(i, carry):
        at = pl.ds(pl.multiple_of(i * pack_rows, pack_rows), pack_rows)
        slot = lax.broadcasted_iota(jnp.int32, (pack_rows, LANES), 1) // HALO
        for side in range(2):
            lanes = slice(0, LANES) if side == 0 else slice(cols - LANES, cols)
            base = 0 if side == 0 else HALO
            first = height_ref[at, lanes]
            coarse = first.astype(jnp.bfloat16).astype(jnp.float32)
            fields = [coarse, first - coarse, rigid_ref[at, lanes], adhes_ref[at, lanes]]
            for s in range(substeps):
                fields.append(force_ref[s, at, lanes].astype(jnp.float32))
            tile = jnp.zeros((pack_rows, LANES), jnp.float32)
            for f, field in enumerate(fields):
                turn = (f * HALO + base) % LANES
                moved = pltpu.roll(field, turn, 1) if turn else field
                tile = jnp.where(slot == f, moved, tile)
            side_send[side, at, :] = tile.astype(jnp.bfloat16)
        return carry

    lax.fori_loop(0, rows // pack_rows, pack, 0)
    pl.semaphore_wait(barrier, 2 + n_col - 1)

    sides = [
        send(side_send.at[k], side_recv.at[k], side_ssem.at[k], side_rsem.at[k], {"col": where})
        for k, where in ((0, left), (1, right))
    ]
    for copy in sides:
        copy.start()

    modes_here = table_x.shape[0] // 2

    def store_x(i, row, cosines, sines):
        lanes = pl.ds(pl.multiple_of(i * cols, cols), cols)
        table_x[row : row + 16, lanes] = cosines.astype(jnp.bfloat16)
        table_x[modes_here + row : modes_here + row + 16, lanes] = (-sines).astype(jnp.bfloat16)

    write_table(cosx_ref, sinx_ref, cols, store_x)

    for copy in sides:
        copy.wait_recv()

    def unpack(i, carry):
        at = pl.ds(pl.multiple_of(i * pack_rows, pack_rows), pack_rows)
        lane = lax.broadcasted_iota(jnp.int32, (pack_rows, LANES), 1)
        after = side_recv[0, at, :].astype(jnp.float32)
        before = side_recv[1, at, :].astype(jnp.float32)
        got = []
        for f in range(4 + substeps):
            turn_a = (-f * HALO) % LANES
            turn_b = (-HALO - f * HALO) % LANES
            a = pltpu.roll(after, turn_a, 1) if turn_a else after
            b = pltpu.roll(before, turn_b, 1) if turn_b else before
            got.append(jnp.where(lane < LANES // 2, a, b))
        inside = pl.ds(pl.multiple_of(i * pack_rows + PAD, 16), pack_rows)
        surf[inside, 0:cols] = height_ref[at, :]
        surf[inside, cols:wide] = got[0] + got[1]
        for f in range(2, 4 + substeps):
            extra[f - 2, at, :] = got[f]
        return carry

    lax.fori_loop(0, rows // pack_rows, unpack, 0)

    def edge_copies(s):
        return [
            send(
                edge_send.at[s, k],
                edge_recv.at[s, k],
                edge_ssem.at[s, k],
                edge_rsem.at[s, k],
                {"row": where},
            )
            for k, where in ((0, up), (1, down))
        ]

    def send_edges(s):
        edge_send[s, 0] = surf[PAD : PAD + 8, :]
        edge_send[s, 1] = surf[PAD + rows - 8 : PAD + rows, :]
        copies = edge_copies(s)
        for copy in copies:
            copy.start()
        return copies

    def bend(start, count):
        block = surf[pl.ds(start - 8, count + 16), :]
        moved_rows = [m[8:-8] for m in shifted(block, 0)]
        middle = block[8:-8]
        moved_cols = shifted(middle, 1)
        slope_r = first_diff(moved_rows)
        slope_c = first_diff(moved_cols)
        metric = 1.0 + (slope_r * slope_r + slope_c * slope_c)
        inverse = lax.rsqrt(metric)
        curv[pl.ds(start, count), :] = (
            second_diff(middle, moved_rows, moved_cols) * (inverse * inverse * inverse)
        )

    def advance(start, count, s):
        inside = pl.ds(start + PAD, count)
        at = pl.ds(start, count)
        block = curv[pl.ds(start + PAD - 8, count + 16), :]
        moved_rows = [m[8:-8] for m in shifted(block, 0)]
        middle = block[8:-8]
        lap = second_diff(middle, moved_rows, shifted(middle, 1))
        rigid = jnp.concatenate([rigid_ref[at, :], extra[0, at, :]], 1)
        adhes = jnp.concatenate([adhes_ref[at, :], extra[1, at, :]], 1)
        noise = jnp.concatenate([force_ref[s, at, :].astype(jnp.float32), extra[2 + s, at, :]], 1)
        center = surf[inside, :]
        binding = adhes * center * jnp.exp(-0.5 * center * center)
        result = center + step_size * (noise - rigid * lap - binding)
        if s < substeps - 1:
            surf[inside, :] = result
        else:
            final = result[:, 0:cols]
            new_ref[at, :] = final
            speed = ((final - height_ref[at, :]) * (1.0 / (substeps * step_size))).astype(
                jnp.bfloat16
            )
            for q in range(chunks):
                vel[q, pl.ds(pl.multiple_of(me_r * rows, rows) + start, count), :] = speed[
                    :, q * LANES : (q + 1) * LANES
                ]

    inner = rows - 32
    strip = next(k for k in (48, 32, 16) if inner % k == 0)

    pending = send_edges(0)
    edges = list(pending)
    for s in range(substeps):

        def bend_strip(i, carry):
            bend(pl.multiple_of(PAD + 16 + i * strip, 16), strip)
            return carry

        def advance_strip(i, carry, s=s):
            advance(pl.multiple_of(16 + i * strip, 16), strip, s)
            return carry

        lax.fori_loop(0, inner // strip, bend_strip, 0)
        for copy in pending:
            copy.wait_recv()
        surf[PAD - 8 : PAD, :] = edge_recv[s, 1]
        surf[PAD + rows : PAD + rows + 8, :] = edge_recv[s, 0]
        bend(PAD - 8, 24)
        bend(PAD + rows - 16, 24)
        advance(0, 16, s)
        advance(rows - 16, 16, s)
        if s < substeps - 1:
            pending = send_edges(s + 1)
            edges += pending
        lax.fori_loop(0, inner // strip, advance_strip, 0)

    def vel_copy(way, distance, q):
        owner = me_r - distance if way == 0 else me_r + distance
        where = down if way == 0 else up
        part = vel.at[q, pl.ds(pl.multiple_of(owner * rows, rows), rows), :]
        sems = (way, distance, q)
        return send(part, part, vel_ssem.at[sems], vel_rsem.at[sems], {"row": where})

    def can_send(way, distance):
        if way == 0:
            return jnp.logical_and(me_r >= distance, me_r + 1 < n_row)
        return jnp.logical_and(me_r + distance < n_row, me_r > 0)

    def has_block(way, distance):
        return me_r >= distance if way == 0 else me_r + distance < n_row

    def vel_arrival(way, distance, q):
        owner = me_r - distance if way == 0 else me_r + distance
        part = vel.at[q, pl.ds(pl.multiple_of(owner * rows, rows), rows), :]
        sems = (way, distance - 1, q)
        where = down if way == 0 else up
        return send(part, part, vel_ssem.at[sems], vel_rsem.at[sems], {"row": where})

    def push(way, distance, q):
        @pl.when(can_send(way, distance))
        def _():
            vel_copy(way, distance, q).start()

    for q in range(chunks):
        for way in range(2):
            push(way, 0, q)

    def store_y(i, row, cosines, sines):
        lanes = pl.ds(pl.multiple_of(i * LANES, LANES), LANES)
        for q in range(chunks):
            part = slice(q * LANES, (q + 1) * LANES)
            table_y[q, row : row + 16, lanes] = cosines[:, part].astype(jnp.bfloat16)
            table_y[q, cols + row : cols + row + 16, lanes] = sines[:, part].astype(jnp.bfloat16)

    write_table(cosy_ref, siny_ref, cols, store_y)

    def mode_part(q, owner):
        return modes.at[q, :, pl.ds(pl.multiple_of(owner * LANES, LANES), LANES)]

    def mode_copy(q, owner, slot, where):
        part = mode_part(q, owner)
        return send(part, part, mode_ssem.at[q, slot], mode_rsem.at[q, slot], {"col": where})

    pairs = n_col // 2
    for q in range(chunks):
        for distance in range(1, n_row):
            for way in range(2):

                @pl.when(has_block(way, distance))
                def _(way=way, distance=distance, q=q):
                    vel_arrival(way, distance, q).wait_recv()

                if distance < n_row - 1:
                    push(way, distance, q)
        result = jnp.dot(table_x[...], vel[q], preferred_element_type=jnp.float32)
        mine = pl.ds(pl.multiple_of(me_c * LANES, LANES), LANES)
        modes[q, :, mine] = result.astype(jnp.bfloat16)
        for off in range(1, pairs):
            mode_copy(q, me_c, pairs - 1 + off, lax.rem(me_c + 2 * off, n_col)).start()
        mode_copy(q, me_c, 0, sibling).start()

    for q in range(chunks):
        for off in range(1, pairs):
            owner = lax.rem(me_c + n_col - 2 * off, n_col)
            mode_copy(q, owner, pairs - 1 + off, sibling).wait_recv()
            mode_copy(q, owner, off, sibling).start()
        mode_copy(q, sibling, 0, sibling).wait_recv()
        for off in range(1, pairs):
            owner = lax.rem(sibling + n_col - 2 * off, n_col)
            mode_copy(q, owner, off, sibling).wait_recv()
        terms = lax.dot_general(
            table_y[q], modes[q], (((1,), (1,)), ((), ())), preferred_element_type=jnp.float32
        )
        k = modes_here
        real = terms[:cols, :k] + terms[cols:, k:]
        imag = terms[:cols, k:] - terms[cols:, :k]
        if q == 0:
            wave_ref[:, :k] = real
            wave_ref[:, k:] = imag
        else:
            wave_ref[:, :k] += real
            wave_ref[:, k:] += imag

    for copy in sides + edges:
        copy.wait_send()
    for q in range(chunks):
        for distance in range(n_row - 1):
            for way in range(2):

                @pl.when(can_send(way, distance))
                def _(way=way, distance=distance, q=q):
                    vel_copy(way, distance, q).wait_send()

        for off in range(1, pairs):
            mode_copy(q, me_c, pairs - 1 + off, lax.rem(me_c + 2 * off, n_col)).wait_send()
            mode_copy(q, me_c, off, sibling).wait_send()
        mode_copy(q, me_c, 0, sibling).wait_send()


def on_device(height, rigidity, adhesion, forcing):
    rows, cols = height.shape
    substeps = forcing.shape[0]
    n_row = lax.axis_size("row")
    n_col = lax.axis_size("col")
    full_rows, full_cols = rows * n_row, cols * n_col
    local_modes = full_rows // 2 // n_row
    chunks = cols // LANES
    pairs = n_col // 2
    wide = cols + LANES
    row_at = lax.axis_index("row") * local_modes
    col_at = lax.axis_index("col") * cols
    cos_x, sin_x = phase_rows(row_at, local_modes, full_rows)
    cos_y, sin_y = phase_rows(col_at, cols, full_cols)
    f32, bf16 = jnp.float32, jnp.bfloat16
    dma = pltpu.SemaphoreType.DMA
    vmem = pl.BlockSpec(memory_space=pltpu.VMEM)
    new_height, waves = pl.pallas_call(
        functools.partial(kernel, substeps, n_row, n_col),
        out_shape=(
            jax.ShapeDtypeStruct((rows, cols), f32),
            jax.ShapeDtypeStruct((cols, 2 * local_modes), f32),
        ),
        in_specs=[vmem] * 8,
        out_specs=(vmem, vmem),
        scratch_shapes=[
            pltpu.VMEM((rows + 2 * PAD, wide), f32),
            pltpu.VMEM((rows + 2 * PAD, wide), f32),
            pltpu.VMEM((2 + substeps, rows, LANES), f32),
            pltpu.VMEM((2, rows, LANES), bf16),
            pltpu.VMEM((2, rows, LANES), bf16),
            pltpu.VMEM((substeps, 2, 8, wide), f32),
            pltpu.VMEM((substeps, 2, 8, wide), f32),
            pltpu.VMEM((2 * local_modes, full_rows), bf16),
            pltpu.VMEM((chunks, 2 * cols, n_col * LANES), bf16),
            pltpu.VMEM((chunks, full_rows, LANES), bf16),
            pltpu.VMEM((chunks, 2 * local_modes, n_col * LANES), bf16),
            dma((2,)),
            dma((2,)),
            dma((substeps, 2)),
            dma((substeps, 2)),
            dma((2, n_row - 1, chunks)),
            dma((2, n_row - 1, chunks)),
            dma((chunks, 2 * pairs - 1)),
            dma((chunks, 2 * pairs - 1)),
        ],
        compiler_params=pltpu.CompilerParams(
            collective_id=0, has_side_effects=True, vmem_limit_bytes=48 * 1024 * 1024
        ),
    )(height, rigidity, adhesion, forcing, cos_x, sin_x, cos_y, sin_y)
    wave_y = col_at + lax.iota(jnp.int32, cols)
    signed = jnp.where(wave_y < full_cols // 2, wave_y, wave_y - full_cols)
    angle_y = signed.astype(f32) * (2.0 * math.pi / full_cols)
    wave_x = row_at + lax.iota(jnp.int32, local_modes)
    angle_x = wave_x.astype(f32) * (2.0 * math.pi / full_rows)
    squared = angle_y[:, None] * angle_y[:, None] + angle_x[None, :] * angle_x[None, :]
    mobility = 1.0 / (2.0 * jnp.sqrt(squared + wave_floor)) / math.sqrt(full_rows * full_cols)
    spectrum = waves.reshape(cols, 2, local_modes) * mobility[:, None, :]
    return (new_height, spectrum)


def solution(mesh):
    in_specs = (
        P(("groups", "row"), "col"),
        P(("groups", "row"), "col"),
        P(("groups", "row"), "col"),
        P(None, ("groups", "row"), "col"),
    )
    out_specs = (P(("groups", "row"), "col"), P(("groups", "col"), None, "row"))
    return jax.shard_map(
        on_device, mesh=mesh, in_specs=in_specs, out_specs=out_specs, check_vma=False
    )
```

time: 142 us -> 61.1 us (0.43)
  Pallas kernels: 0 us -> 53 us
  waiting for transfers between devices: 49.6 us -> 0 us
  other arithmetic: 37.1 us -> 2.66 us
  local copies, waits for them, and re-layouts: 18.5 us -> 4.44 us
  between operations: 14.4 us -> 0.72 us
  starting transfers between devices: 13.5 us -> 0 us
  matrix products: 7.34 us -> 0 us
    pallas_call x0 -> x1, Pallas kernels: none -> 53 us  [on_device(): pl.pallas_call(functools.partial(kernel, substeps, n_row, n_col), out_sha...]
    reduce_scatter x1 -> x0, waiting for transfers between devices: 31.4 us -> none  [on_device(): lax.psum_scatter(wave_terms(jnp.int32(0), local_cols * lax.axis_size('col...]
    all_to_all x2 -> x0, waiting for transfers between devices: 15.7 us -> none  [the longest x1 8.82 us: on_device(): lax.all_to_all(velocity, 'row', split_axis=1, concat_axis=0, tiled=True)]
    add x6 -> x1, other arithmetic: 7.84 us -> 0.01 us  [phase_rows(): start + 64 * lax.iota(jnp.int32, modes // 64)]
    dot_general x6 -> x0, matrix products: 7.34 us -> none  [the longest x2 4.85 us: on_device(): lax.dot_general(columns, cosines, (((0,), (1,)), ((), ())), preferred_ele...]
    convert_element_type x4 -> x0, other arithmetic: 7.34 us -> none  [the longest x2 4.84 us: phase_table(): return (cosines.astype(jnp.bfloat16), sines.astype(jnp.bfloat16))]
    div x4 -> x0, other arithmetic: 7.01 us -> none  [substep(): curvature = lap_four(padded) / (metric * jnp.sqrt(metric))]
    all_to_all x2 -> x0, starting transfers between devices: 6.95 us -> none  [the longest x1 3.54 us: on_device(): lax.all_to_all(velocity, 'row', split_axis=1, concat_axis=0, tiled=True)]
  transfers between devices with their start and end apart: 7 -> 0, of which waited for: 5 -> 0; matrix products, arithmetic and copies ran while one was open for 10% -> 0% of each run, Pallas kernels for 0% -> 0%
where the time goes in v1:
time: 61.1 us; the launch traced here: 60.9 us
  Pallas kernels  53 us (87%)
  local copies, waits for them, and re-layouts  4.44 us (7%)
  other arithmetic  2.66 us (4%)
  between operations  0.72 us (1%)
    pallas_call x1, Pallas kernels, on_device(): pl.pallas_call(functools.partial(kernel, substeps, n_row, n_col), out_sha...  53 us
    unnamed x9, local copies, waits for them, and re-layouts  4.1 us
    sin x2, other arithmetic, phase_rows(): return (jnp.cos(angle), jnp.sin(angle))  1.31 us

profile of v1, /device:TPU:1, one launch (start us, length us, event | category | flops | bytes accessed | tf_op | source)
XLA Modules:
  0.0 60.9 jit_solution(13768390488979931266)
XLA Ops:
  0.6 0.0 copy-start.1
  0.7 0.1 pad_add_fusion.2
  0.8 0.8 %fusion.11 = (f32[20,2048]{1,0:T(8,128)S(1)}, f32[20,2048]{1,0:T(8,128)S(1)}) fusion(s32[20]{0:T(128)S(1)} %get-tuple-element.7), kind=kLoop, calls=%fused_computation.19 | loop fusion | flops 573440 | bytes 327760 | tf_op jit(solution)/shard_map/sin | solution.py:30
  1.6 0.5 fusion.14
  2.1 0.0 copy-done.1
  2.1 0.0 copy-start
  2.1 1.2 %copy-done = bf16[4,512,256]{2,1,0:T(8,128)(2,1)S(1)} copy-done((bf16[4,512,256]{2,1,0:T(8,128)(2,1)S(1)}, bf16[4,512,256]{2,1,0:T(8,128)(2,1)}, u32[]{:S(2)}) %copy-start) | copy-done | bytes 1048600
  3.3 0.0 copy-start.2
  3.3 1.0 %copy-done.2 = f32[512,256]{1,0:T(8,128)S(1)} copy-done((f32[512,256]{1,0:T(8,128)S(1)}, f32[512,256]{1,0:T(8,128)}, u32[]{:S(2)}) %copy-start.2) | copy-done | bytes 524312
  4.4 0.0 copy-start.3
  4.4 1.0 %copy-done.3 = f32[512,256]{1,0:T(8,128)S(1)} copy-done((f32[512,256]{1,0:T(8,128)S(1)}, f32[512,256]{1,0:T(8,128)}, u32[]{:S(2)}) %copy-start.3) | copy-done | bytes 524312
  5.4 53.0 %shard_map.59 = (f32[512,256]{1,0:T(8,128)S(1)}, f32[256,512]{1,0:T(8,128)S(1)}) custom-call(f32[512,256]{1,0:T(8,128)S(1)} %copy-done.1, f32[512,256]{1,0:T(8,128)S(1)} %copy-done.2, f32[512,256]{1,0:T(8,128)S(1)} %copy-done.3, bf16[4,512,256]{2,1,0:T(8,128)(2,1)S(1)} %copy-done, f32[20,2048]{1,0:T(8,128)S(1)} %get-tuple-element.11.cosx_ref, ...), custom_call_target="tpu_custom_call" | custom-call | tf_op jit(solution)/shard_map/pallas_call | solution.py:410
  58.5 0.3 reshape.56
  58.8 0.2 divide_multiply_fusion
  59.0 1.1 %broadcast_multiply_fusion = f32[256,2,256]{2,1,0:T(2,128)} fusion(f32[256,2,256]{2,1,0:T(2,128)S(1)} %reshape.56, f32[256,256]{1,0:T(8,128)S(1)} %divide_multiply_fusion), kind=kLoop, calls=%fused_computation.3 | loop fusion | flops 131072 | bytes 1310720 | tf_op jit(solution)/shard_map/mul | solution.py:450
  60.1 0.8 %copy.7 = f32[512,256]{1,0:T(8,128)} copy(f32[512,256]{1,0:T(8,128)S(1)} %get-tuple-element.18) | data formatting | bytes 1048576
  (4 shorter events, 0.0 us)
Async XLA Ops:
  0.6 1.4 %copy-start.1 = (f32[512,256]{1,0:T(8,128)S(1)}, f32[512,256]{1,0:T(8,128)}, u32[]{:S(2)}) copy-start(f32[512,256]{1,0:T(8,128)} %height_ref.1) | copy-start | bytes 1572868
  2.1 1.2 %copy-start = (bf16[4,512,256]{2,1,0:T(8,128)(2,1)S(1)}, bf16[4,512,256]{2,1,0:T(8,128)(2,1)}, u32[]{:S(2)}) copy-start(bf16[4,512,256]{2,1,0:T(8,128)(2,1)} %force_ref.1) | copy-start | bytes 3145732
  3.3 1.0 %copy-start.2 = (f32[512,256]{1,0:T(8,128)S(1)}, f32[512,256]{1,0:T(8,128)}, u32[]{:S(2)}) copy-start(f32[512,256]{1,0:T(8,128)} %rigid_ref.1) | copy-start | bytes 1572868
  4.4 1.0 %copy-start.3 = (f32[512,256]{1,0:T(8,128)S(1)}, f32[512,256]{1,0:T(8,128)}, u32[]{:S(2)}) copy-start(f32[512,256]{1,0:T(8,128)} %adhes_ref.1) | copy-start | bytes 1572868

commit v2 on v1

--- a/solution.py
+++ b/solution.py
@@ -16,28 +16,46 @@
 PAD = 16
 
 
-def phase_rows(start, modes, period):
-    ks = jnp.concatenate(
-        [
-            8 * lax.iota(jnp.int32, 8),
-            lax.iota(jnp.int32, 8),
-            start + 64 * lax.iota(jnp.int32, modes // 64),
-        ]
-    )
-    angle = (ks[:, None] * lax.iota(jnp.int32, period)[None, :] % period).astype(jnp.float32) * (
-        2.0 * math.pi / period
-    )
-    return jnp.cos(angle), jnp.sin(angle)
-
-
-def write_table(cos_ref, sin_ref, width, store):
+def write_phases(start, cos_ref, sin_ref):
     rows, period = cos_ref.shape
+    width = 2 * LANES
+
+    def columns(i, carry):
+        at = pl.multiple_of(i * width, width)
+        for top in range(0, rows, 8):
+            k = lax.broadcasted_iota(jnp.int32, (8, width), 0)
+            if top == 0:
+                k = 8 * k
+            elif top >= 16:
+                k = start + 64 * (top - 16 + k)
+            turn = lax.rem(k * (at + lax.broadcasted_iota(jnp.int32, (8, width), 1)), period)
+            quarter = jnp.zeros_like(turn)
+            for edge in (1, 3, 5, 7):
+                quarter += (turn >= edge * period // 8).astype(jnp.int32)
+            x = (turn - quarter * (period // 4)).astype(jnp.float32) * (2.0 * math.pi / period)
+            y = x * x
+            sine = x * (1.0 + y * (-1 / 6 + y * (1 / 120 + y * (-1 / 5040 + y * (1 / 362880)))))
+            cosine = 1.0 + y * (-1 / 2 + y * (1 / 24 + y * (-1 / 720 + y * (1 / 40320))))
+            odd = jnp.logical_or(quarter == 1, quarter == 3)
+            first = jnp.where(odd, sine, cosine)
+            second = jnp.where(odd, cosine, sine)
+            minus_cos = jnp.logical_or(quarter == 1, quarter == 2)
+            minus_sin = jnp.logical_or(quarter == 2, quarter == 3)
+            cos_ref[top : top + 8, pl.ds(at, width)] = jnp.where(minus_cos, -first, first)
+            sin_ref[top : top + 8, pl.ds(at, width)] = jnp.where(minus_sin, -second, second)
+        return carry
+
+    lax.fori_loop(0, period // width, columns, 0)
+
+
+def write_table(cos_ref, sin_ref, coarse, width, store):
+    period = cos_ref.shape[1]
 
     def columns(i, carry):
         lanes = pl.ds(pl.multiple_of(i * width, width), width)
         cos_c, sin_c = cos_ref[0:8, lanes], sin_ref[0:8, lanes]
         cos_b, sin_b = cos_ref[8:16, lanes], sin_ref[8:16, lanes]
-        for a in range(rows - 16):
+        for a in range(coarse):
             cos_a, sin_a = cos_ref[16 + a : 17 + a, lanes], sin_ref[16 + a : 17 + a, lanes]
             cos_ac = cos_a * cos_c - sin_a * sin_c
             sin_ac = sin_a * cos_c + cos_a * sin_c
@@ -72,16 +90,21 @@
     substeps,
     n_row,
     n_col,
+    height_in,
+    rigid_in,
+    adhes_in,
+    force_in,
+    new_out,
+    wave_ref,
     height_ref,
     rigid_ref,
     adhes_ref,
     force_ref,
+    new_ref,
     cosx_ref,
     sinx_ref,
     cosy_ref,
     siny_ref,
-    new_ref,
-    wave_ref,
     surf,
     curv,
     extra,
@@ -101,6 +124,8 @@
     vel_rsem,
     mode_ssem,
     mode_rsem,
+    load_sem,
+    out_sem,
 ):
     rows, cols = height_ref.shape
     chunks = cols // LANES
@@ -114,6 +139,20 @@
     sibling = me_c + 1 - 2 * lax.rem(me_c, 2)
     mesh_ids = pl.DeviceIdType.MESH
 
+    loads = [
+        pltpu.make_async_copy(src, dst, load_sem.at[i])
+        for i, (src, dst) in enumerate(
+            (
+                (height_in, height_ref),
+                (rigid_in, rigid_ref),
+                (adhes_in, adhes_ref),
+                (force_in, force_ref),
+            )
+        )
+    ]
+    for copy in loads:
+        copy.start()
+
     barrier = pltpu.get_barrier_semaphore()
     for target in (down, up):
         pl.semaphore_signal(barrier, inc=1, device_id={"row": target}, device_id_type=mesh_ids)
@@ -136,6 +175,8 @@
         )
 
     pack_rows = 32
+    for copy in loads:
+        copy.wait()
 
     def pack(i, carry):
         at = pl.ds(pl.multiple_of(i * pack_rows, pack_rows), pack_rows)
@@ -173,7 +214,8 @@
         table_x[row : row + 16, lanes] = cosines.astype(jnp.bfloat16)
         table_x[modes_here + row : modes_here + row + 16, lanes] = (-sines).astype(jnp.bfloat16)
 
-    write_table(cosx_ref, sinx_ref, cols, store_x)
+    write_phases(me_r * modes_here, cosx_ref, sinx_ref)
+    write_table(cosx_ref, sinx_ref, modes_here // 64, cols, store_x)
 
     for copy in sides:
         copy.wait_recv()
@@ -259,7 +301,7 @@
                 ]
 
     inner = rows - 32
-    strip = next(k for k in (48, 32, 16) if inner % k == 0)
+    strip = next(k for k in (96, 48, 32, 16) if inner % k == 0)
 
     pending = send_edges(0)
     edges = list(pending)
@@ -317,6 +359,8 @@
     for q in range(chunks):
         for way in range(2):
             push(way, 0, q)
+    result_out = pltpu.make_async_copy(new_ref, new_out, out_sem)
+    result_out.start()
 
     def store_y(i, row, cosines, sines):
         lanes = pl.ds(pl.multiple_of(i * LANES, LANES), LANES)
@@ -325,7 +369,8 @@
             table_y[q, row : row + 16, lanes] = cosines[:, part].astype(jnp.bfloat16)
             table_y[q, cols + row : cols + row + 16, lanes] = sines[:, part].astype(jnp.bfloat16)
 
-    write_table(cosy_ref, siny_ref, cols, store_y)
+    write_phases(me_c * cols, cosy_ref, siny_ref)
+    write_table(cosy_ref, siny_ref, cols // 64, cols, store_y)
 
     def mode_part(q, owner):
         return modes.at[q, :, pl.ds(pl.multiple_of(owner * LANES, LANES), LANES)]
@@ -374,6 +419,7 @@
             wave_ref[:, :k] += real
             wave_ref[:, k:] += imag
 
+    result_out.wait()
     for copy in sides + edges:
         copy.wait_send()
     for q in range(chunks):
@@ -402,10 +448,11 @@
     wide = cols + LANES
     row_at = lax.axis_index("row") * local_modes
     col_at = lax.axis_index("col") * cols
-    cos_x, sin_x = phase_rows(row_at, local_modes, full_rows)
-    cos_y, sin_y = phase_rows(col_at, cols, full_cols)
+    rows_x = 16 + -(-local_modes // 512) * 8
+    rows_y = 16 + -(-cols // 512) * 8
     f32, bf16 = jnp.float32, jnp.bfloat16
     dma = pltpu.SemaphoreType.DMA
+    hbm = pl.BlockSpec(memory_space=pltpu.HBM)
     vmem = pl.BlockSpec(memory_space=pltpu.VMEM)
     new_height, waves = pl.pallas_call(
         functools.partial(kernel, substeps, n_row, n_col),
@@ -413,9 +460,18 @@
             jax.ShapeDtypeStruct((rows, cols), f32),
             jax.ShapeDtypeStruct((cols, 2 * local_modes), f32),
         ),
-        in_specs=[vmem] * 8,
-        out_specs=(vmem, vmem),
+        in_specs=[hbm] * 4,
+        out_specs=(hbm, vmem),
         scratch_shapes=[
+            pltpu.VMEM((rows, cols), f32),
+            pltpu.VMEM((rows, cols), f32),
+            pltpu.VMEM((rows, cols), f32),
+            pltpu.VMEM((substeps, rows, cols), bf16),
+            pltpu.VMEM((rows, cols), f32),
+            pltpu.VMEM((rows_x, full_rows), f32),
+            pltpu.VMEM((rows_x, full_rows), f32),
+            pltpu.VMEM((rows_y, full_cols), f32),
+            pltpu.VMEM((rows_y, full_cols), f32),
             pltpu.VMEM((rows + 2 * PAD, wide), f32),
             pltpu.VMEM((rows + 2 * PAD, wide), f32),
             pltpu.VMEM((2 + substeps, rows, LANES), f32),
@@ -435,11 +491,13 @@
             dma((2, n_row - 1, chunks)),
             dma((chunks, 2 * pairs - 1)),
             dma((chunks, 2 * pairs - 1)),
+            dma((4,)),
+            dma,
         ],
         compiler_params=pltpu.CompilerParams(
-            collective_id=0, has_side_effects=True, vmem_limit_bytes=48 * 1024 * 1024
+            collective_id=0, has_side_effects=True, vmem_limit_bytes=127 * 512 * 1024
         ),
-    )(height, rigidity, adhesion, forcing, cos_x, sin_x, cos_y, sin_y)
+    )(height, rigidity, adhesion, forcing)
     wave_y = col_at + lax.iota(jnp.int32, cols)
     signed = jnp.where(wave_y < full_cols // 2, wave_y, wave_y - full_cols)
     angle_y = signed.astype(f32) * (2.0 * math.pi / full_cols)

time: 61.1 us -> 58.2 us (0.953)
  local copies, waits for them, and re-layouts: 4.44 us -> 2.17 us
  other arithmetic: 2.66 us -> 1.26 us
  Pallas kernels: 53 us -> 53.9 us
    unnamed x9 -> x3, local copies, waits for them, and re-layouts: 4.1 us -> 0.8 us
    sin x2 -> x0, other arithmetic: 1.31 us -> none  [phase_rows(): return (jnp.cos(angle), jnp.sin(angle))]
    reshape x1, local copies, waits for them, and re-layouts: 0.34 us -> 1.37 us  [on_device(): spectrum = waves.reshape(cols, 2, local_modes) * mobility[:, None, :]]
    pallas_call x1, Pallas kernels: 53 us -> 53.9 us  [on_device(): pl.pallas_call(functools.partial(kernel, substeps, n_row, n_col), out_sha...]
where the time goes in v2:
time: 58.2 us; the launch traced here: 58 us
  Pallas kernels  53.9 us (93%)
  local copies, waits for them, and re-layouts  2.17 us (4%)
  other arithmetic  1.26 us (2%)
  between operations  0.67 us (1%)
    pallas_call x1, Pallas kernels, on_device(): pl.pallas_call(functools.partial(kernel, substeps, n_row, n_col), out_sha...  53.9 us
    reshape x1, local copies, waits for them, and re-layouts, on_device(): spectrum = waves.reshape(cols, 2, local_modes) * mobility[:, None, :]  1.37 us

profile of v2, /device:TPU:1, one launch (start us, length us, event | category | flops | bytes accessed | tf_op | source)
XLA Modules:
  0.0 58.0 jit_solution(1539070618520770074)
XLA Ops:
  0.6 53.9 %shard_map.59 = (f32[512,256]{1,0:T(8,128)}, f32[256,512]{1,0:T(8,128)}) custom-call(f32[512,256]{1,0:T(8,128)} %height_in.1, f32[512,256]{1,0:T(8,128)} %rigid_in.1, f32[512,256]{1,0:T(8,128)} %adhes_in.1, bf16[4,512,256]{2,1,0:T(8,128)(2,1)} %force_in.1), custom_call_target="tpu_custom_call" | custom-call | tf_op jit(solution)/shard_map/pallas_call | solution.py:457
  54.5 1.4 %reshape.54 = f32[256,2,256]{2,1,0:T(2,128)S(1)} reshape(f32[256,512]{1,0:T(8,128)} %get-tuple-element.5) | data formatting | bytes 1048576 | tf_op jit(solution)/shard_map/reshape | solution.py:508
  55.9 0.2 divide_multiply_fusion
  56.1 0.0 copy-start
  56.1 1.1 %broadcast_multiply_fusion = f32[256,2,256]{2,1,0:T(2,128)} fusion(f32[256,2,256]{2,1,0:T(2,128)S(1)} %reshape.54, f32[256,256]{1,0:T(8,128)S(1)} %divide_multiply_fusion), kind=kLoop, calls=%fused_computation | loop fusion | flops 131072 | bytes 1310720 | tf_op jit(solution)/shard_map/mul | solution.py:508
  57.2 0.0 copy-done
  57.2 0.8 %copy.7 = f32[512,256]{1,0:T(8,128)} copy(f32[512,256]{1,0:T(8,128)S(1)} %copy-done) | data formatting | bytes 1048576
  (1 shorter events, 0.0 us)
Async XLA Ops:
  56.1 1.1 %copy-start = (f32[512,256]{1,0:T(8,128)S(1)}, f32[512,256]{1,0:T(8,128)}, u32[]{:S(2)}) copy-start(f32[512,256]{1,0:T(8,128)} %get-tuple-element.10) | copy-start | bytes 1572868

commit v3 on v2

--- a/solution.py
+++ b/solution.py
@@ -303,6 +303,18 @@
     inner = rows - 32
     strip = next(k for k in (96, 48, 32, 16) if inner % k == 0)
 
+    def send_own(start, count):
+        for q in range(chunks):
+            part = vel.at[q, pl.ds(pl.multiple_of(me_r * rows + start, 16), count), :]
+            for way, where in ((0, down), (1, up)):
+
+                @pl.when(me_r + 1 < n_row if way == 0 else me_r > 0)
+                def _(part=part, way=way, where=where, q=q):
+                    sems = (way, 0, q)
+                    send(
+                        part, part, vel_ssem.at[sems], vel_rsem.at[sems], {"row": where}
+                    ).start()
+
     pending = send_edges(0)
     edges = list(pending)
     for s in range(substeps):
@@ -327,7 +339,15 @@
         if s < substeps - 1:
             pending = send_edges(s + 1)
             edges += pending
-        lax.fori_loop(0, inner // strip, advance_strip, 0)
+        if s < substeps - 1:
+            lax.fori_loop(0, inner // strip, advance_strip, 0)
+            continue
+        some = inner // strip * 2 // 5
+        lax.fori_loop(0, some, advance_strip, 0)
+        cut = 16 + some * strip
+        send_own(0, cut)
+        lax.fori_loop(some, inner // strip, advance_strip, 0)
+        send_own(cut, rows - cut)
 
     def vel_copy(way, distance, q):
         owner = me_r - distance if way == 0 else me_r + distance
@@ -356,9 +376,6 @@
         def _():
             vel_copy(way, distance, q).start()
 
-    for q in range(chunks):
-        for way in range(2):
-            push(way, 0, q)
     result_out = pltpu.make_async_copy(new_ref, new_out, out_sem)
     result_out.start()
 

time: 58.2 us -> 58.4 us (level)
  no operation moved by 1% of the time
where the time goes in v3:
time: 58.4 us; the launch traced here: 58.2 us
  Pallas kernels  54.1 us (93%)
  local copies, waits for them, and re-layouts  2.17 us (4%)
  other arithmetic  1.26 us (2%)
  between operations  0.67 us (1%)
    pallas_call x1, Pallas kernels, on_device(): pl.pallas_call(functools.partial(kernel, substeps, n_row, n_col), out_sha...  54.1 us
    reshape x1, local copies, waits for them, and re-layouts, on_device(): spectrum = waves.reshape(cols, 2, local_modes) * mobility[:, None, :]  1.37 us

profile of v3, /device:TPU:1, one launch (start us, length us, event | category | flops | bytes accessed | tf_op | source)
XLA Modules:
  0.0 58.2 jit_solution(17121816435140022893)
XLA Ops:
  0.6 54.1 %shard_map.59 = (f32[512,256]{1,0:T(8,128)}, f32[256,512]{1,0:T(8,128)}) custom-call(f32[512,256]{1,0:T(8,128)} %height_in.1, f32[512,256]{1,0:T(8,128)} %rigid_in.1, f32[512,256]{1,0:T(8,128)} %adhes_in.1, bf16[4,512,256]{2,1,0:T(8,128)(2,1)} %force_in.1), custom_call_target="tpu_custom_call" | custom-call | tf_op jit(solution)/shard_map/pallas_call | solution.py:474
  54.8 1.4 %reshape.54 = f32[256,2,256]{2,1,0:T(2,128)S(1)} reshape(f32[256,512]{1,0:T(8,128)} %get-tuple-element.5) | data formatting | bytes 1048576 | tf_op jit(solution)/shard_map/reshape | solution.py:525
  56.2 0.2 divide_multiply_fusion
  56.4 0.0 copy-start
  56.4 1.1 %broadcast_multiply_fusion = f32[256,2,256]{2,1,0:T(2,128)} fusion(f32[256,2,256]{2,1,0:T(2,128)S(1)} %reshape.54, f32[256,256]{1,0:T(8,128)S(1)} %divide_multiply_fusion), kind=kLoop, calls=%fused_computation | loop fusion | flops 131072 | bytes 1310720 | tf_op jit(solution)/shard_map/mul | solution.py:525
  57.4 0.0 copy-done
  57.4 0.8 %copy.7 = f32[512,256]{1,0:T(8,128)} copy(f32[512,256]{1,0:T(8,128)S(1)} %copy-done) | data formatting | bytes 1048576
  (1 shorter events, 0.0 us)
Async XLA Ops:
  56.4 1.1 %copy-start = (f32[512,256]{1,0:T(8,128)S(1)}, f32[512,256]{1,0:T(8,128)}, u32[]{:S(2)}) copy-start(f32[512,256]{1,0:T(8,128)} %get-tuple-element.10) | copy-start | bytes 1572868
